TPU v7x, 32 devices: a whole 2x2x4 slice. The times are simulated.
32 devices in a mesh: seq: 16 (over z, x, core), head: 2 (over y).
Axes of the slice: x: 2, y: 2, z: 4, core: 2. Of those that a mesh axis runs over, the one named last changes fastest.
Arguments:
- queries: bfloat16 [12288, 2048], P(('seq', 'head')), may hold values from -6 to 6
- keys: bfloat16 [12288, 2048], P(('seq', 'head')), may hold values from -6 to 6
- values: bfloat16 [12288, 2048], P(('seq', 'head')), may hold values from -6 to 6
- out_grad: bfloat16 [12288, 2048], P(('seq', 'head')), may hold values from -6 to 6
- window: int32 [16, 2], replicated, may hold values from 0 to 1, as said below
Outputs:
- grad_queries: bfloat16 [12288, 2048], P(('seq', 'head'))
- grad_keys: bfloat16 [12288, 2048], P(('seq', 'head'))
- grad_values: bfloat16 [12288, 2048], P(('seq', 'head'))
Inputs may be any that keep to these rules, and one draw needn't show every extreme that they name: `window`: some head reaches 1 along both time and height, some head 0 along both.
All inputs are finite; a program needn't handle non-finite values.
Results may differ from a plain program's by a relative error of at most 0.0066.
Values may be sent and summed in bfloat16 or wider, within the bound.
A program may use at most 192 MiB of HBM per device.

v0:
```python
import functools

import jax
import jax.numpy as jnp
from jax import lax
from jax.experimental import pallas as pl
from jax.experimental.pallas import tpu as pltpu
from jax.sharding import PartitionSpec as P

HD = 128
GH = 4
SCALE = HD ** (-0.5)
LOG2E = 1.4426950408889634
MESH = pl.DeviceIdType.MESH


def visible_slots(window, heads_here):
    seq_index = lax.axis_index("seq")
    grid_time = 2 * (lax.axis_size("seq") // GH)
    reaches = lax.dynamic_slice_in_dim(window, lax.axis_index("head") * heads_here, heads_here, 0)
    slot = jnp.arange(9)
    time_off, row_off = slot // 3 - 1, slot % 3 - 1
    near_time = 2 * (seq_index // GH) + jnp.arange(2)[:, None] + time_off[None, :]
    near_row = seq_index % GH + row_off
    inside = (near_time >= 0) & (near_time < grid_time)
    inside = inside & ((near_row >= 0) & (near_row < GH))[None, :]
    reach = (jnp.abs(time_off)[None, :] <= reaches[:, :1]) & (
        jnp.abs(row_off)[None, :] <= reaches[:, 1:]
    )
    return (inside[None] & reach[:, None, :]).astype(jnp.int32).reshape(-1)


def dot(a, b, dims):
    return lax.dot_general(a, b, (dims, ((), ())), preferred_element_type=jnp.float32)


def attend_kernel(
    vis_ref, q_ref, g_ref, kv_ref, dq_ref, dkv_ref, e_scr, dp_scr, acc, dqt, tops, top, total, delta
):
    head = pl.program_id(0)
    tile = q_ref.shape[1] // 2

    def seen(qt, row, time):
        step = time - qt
        inside = jnp.logical_and(step >= 0, step < 3)
        slot = jnp.clip(step, 0, 2) * 3 + row
        return jnp.logical_and(inside, vis_ref[(head * 2 + qt) * 9 + slot] == 1)

    def one_tile(qt, carry):
        rows = pl.ds(pl.multiple_of(qt * tile, tile), tile)
        q = q_ref[0, rows, :]
        g = g_ref[0, rows, :]
        top[...] = jnp.full_like(top, -jnp.inf)
        total[...] = jnp.zeros_like(total)
        delta[...] = jnp.zeros_like(delta)
        dqt[...] = jnp.zeros_like(dqt)

        def over_visible(body):
            def step(slot, carry):
                @pl.when(vis_ref[(head * 2 + qt) * 9 + slot] == 1)
                def _():
                    body(slot, lax.rem(slot, 3), qt + lax.div(slot, 3))

                return carry

            lax.fori_loop(0, 9, step, 0)

        def scores(slot, row, time):
            s = dot(kv_ref[0, 0, row, time], q, ((1,), (1,)))
            old = top[...]
            new = jnp.maximum(old, jnp.max(s, axis=0, keepdims=True))
            shrink = jnp.exp2((old - new) * (SCALE * LOG2E))
            dp = dot(kv_ref[0, 1, row, time], g, ((1,), (1,)))
            e = jnp.exp2((s - new) * (SCALE * LOG2E))
            e_scr[slot] = e
            dp_scr[slot] = dp
            tops[slot] = new
            top[...] = new
            total[...] = total[...] * shrink + jnp.sum(e, axis=0, keepdims=True)
            delta[...] = delta[...] * shrink + jnp.sum(e * dp, axis=0, keepdims=True)

        def grads(slot, row, time):
            @pl.when(jnp.logical_or(qt == 0, jnp.logical_not(seen(0, row, time))))
            def _():
                acc[:, row, time] = jnp.zeros((2,) + acc.shape[3:], jnp.float32)

            p = e_scr[slot] * (jnp.exp2((tops[slot] - top[...]) * (SCALE * LOG2E)) * total[...])
            ds = (p * (dp_scr[slot] - delta[...])).astype(jnp.bfloat16)
            acc[1, row, time] += dot(p.astype(jnp.bfloat16), g, ((1,), (0,)))
            acc[0, row, time] += dot(ds, q, ((1,), (0,)))
            dqt[...] += dot(kv_ref[0, 0, row, time], ds, ((0,), (0,)))

        over_visible(scores)
        total[...] = 1.0 / total[...]
        delta[...] = delta[...] * total[...]
        over_visible(grads)
        dq_ref[0, rows, :] = (dqt[...] * SCALE).T.astype(jnp.bfloat16)
        return carry

    lax.fori_loop(0, 2, one_tile, 0)

    def hand_out(index, carry):
        row, time = lax.div(index, 4), lax.rem(index, 4)
        used = jnp.logical_or(seen(0, row, time), seen(1, row, time))

        @pl.when(used)
        def _():
            dkv_ref[0, 0, row, time] = (acc[0, row, time] * SCALE).astype(jnp.bfloat16)
            dkv_ref[0, 1, row, time] = acc[1, row, time].astype(jnp.bfloat16)

        @pl.when(jnp.logical_not(used))
        def _():
            dkv_ref[0, :, row, time] = jnp.zeros((2,) + acc.shape[3:], jnp.bfloat16)

        return carry

    lax.fori_loop(0, 12, hand_out, 0)


def attend(vis, q, g, kv):
    heads, rows, _ = q.shape
    tile = rows // 2
    by_head = lambda shape: pl.BlockSpec(
        (1,) + shape, lambda n, vis: (n,) + (0,) * len(shape)
    )
    pairs = heads * 18
    return pl.pallas_call(
        attend_kernel,
        grid_spec=pltpu.PrefetchScalarGridSpec(
            num_scalar_prefetch=1,
            grid=(heads,),
            in_specs=[
                by_head((rows, HD)),
                by_head((rows, HD)),
                by_head((2, 3, 4, tile, HD)),
            ],
            out_specs=[by_head((rows, HD)), by_head((2, 3, 4, tile, HD))],
            scratch_shapes=[
                pltpu.VMEM((9, tile, tile), jnp.float32),
                pltpu.VMEM((9, tile, tile), jnp.float32),
                pltpu.VMEM((2, 3, 4, tile, HD), jnp.float32),
                pltpu.VMEM((HD, tile), jnp.float32),
                pltpu.VMEM((9, 1, tile), jnp.float32),
                pltpu.VMEM((1, tile), jnp.float32),
                pltpu.VMEM((1, tile), jnp.float32),
                pltpu.VMEM((1, tile), jnp.float32),
            ],
        ),
        out_shape=[
            jax.ShapeDtypeStruct(q.shape, jnp.bfloat16),
            jax.ShapeDtypeStruct(kv.shape, jnp.bfloat16),
        ],
        compiler_params=pltpu.CompilerParams(
            dimension_semantics=("arbitrary",), vmem_limit_bytes=48 * 2**20
        ),
        cost_estimate=pl.CostEstimate(
            flops=pairs * 5 * tile * tile * HD,
            bytes_accessed=4 * kv.size + 6 * q.size,
            transcendentals=pairs * tile * tile // 2,
        ),
        name="attend",
    )(vis, q, g, kv)


def neighbours():
    seq = lax.axis_index("seq")
    row, slab = lax.rem(seq, GH), lax.div(seq, GH)
    slabs = lax.axis_size("seq") // GH
    return (
        (row > 0, seq - 1),
        (row < GH - 1, seq + 1),
        (slab > 0, seq - GH),
        (slab < slabs - 1, seq + GH),
    )


def far_row():
    row = lax.rem(lax.axis_index("seq"), GH)
    odd = lax.rem(row, 2)
    exists = jnp.where(odd == 1, row < GH - 1, row > 0)
    return exists, 2 * odd


def greet(partners, peers):
    barrier = pltpu.get_barrier_semaphore()
    for peer in peers:
        pl.semaphore_signal(barrier, inc=1, device_id={"head": peer}, device_id_type=MESH)
    for exists, seq in partners:

        @pl.when(exists)
        def _():
            pl.semaphore_signal(barrier, inc=1, device_id={"seq": seq}, device_id_type=MESH)

    count = sum(exists.astype(jnp.int32) for exists, _ in partners)
    pl.semaphore_wait(barrier, count + len(peers))


def remote(src, dst, sems, index, device):
    return pltpu.make_async_remote_copy(
        src_ref=src,
        dst_ref=dst,
        send_sem=sems[0].at[index],
        recv_sem=sems[1].at[index],
        device_id=device,
        device_id_type=MESH,
    )


def for_heads(heads, body):
    def step(n, carry):
        body(n)
        return carry

    lax.fori_loop(0, heads, step, 0)


def gather_kernel(
    nh, q_in, k_in, v_in, g_in, q_out, g_out, kv_out, own, swap_s, swap_r, near_s, near_r
):
    heads, _, _, _, tile, _ = kv_out.shape
    rows = q_in.shape[0]
    h = lax.axis_index("head")
    partners = neighbours()
    up, down, before, after = partners
    peers = [lax.rem(h + j, nh) for j in range(1, nh)]
    senders = [lax.rem(h + nh - j, nh) for j in range(1, nh)]
    sources = (k_in, v_in, q_in, g_in)
    far_exists, far = far_row()
    share = nh // 2

    def place(array, n, owner):
        if array < 2:
            offset = pl.multiple_of(lax.rem(owner, share) * rows, rows)
            return kv_out.at[n, array, 1, 1 + lax.div(owner, share), pl.ds(offset, rows)]
        out = q_out if array == 2 else g_out
        return out.at[n, pl.ds(pl.multiple_of(owner * rows, rows), rows)]

    def columns(array, n, owner):
        start = pl.multiple_of((owner * heads + n) * HD, HD)
        return sources[array].at[:, pl.ds(start, HD)]

    def kept(array, n):
        return pltpu.make_async_copy(columns(array, n, h), place(array, n, h), own.at[array, n])

    def swapped(array, n, j, owner):
        return remote(
            columns(array, n, peers[j]),
            place(array, n, owner),
            (swap_s, swap_r),
            (array, j, n),
            {"head": peers[j]},
        )

    def start_swap(arrays, n):
        for array in arrays:
            for j in range(nh - 1):
                swapped(array, n, j, h).start()
            kept(array, n).start()

    def wait_swap(arrays, n):
        for array in arrays:
            for j in range(nh - 1):
                swapped(array, n, j, senders[j]).wait_recv()
            kept(array, n).wait()

    def block(n, row, first, count):
        return kv_out.at[n, :, row, pl.ds(first, count)]

    def copies(kind, n):
        if kind == 0:
            mine, plan = (1, 1, 2), ((up, (2, 1, 2), (0, 1, 2)), (down, (0, 1, 2), (2, 1, 2)))
        elif kind == 1:
            plan = ((before, (1, 3, 1), (1, 0, 1)), (after, (1, 0, 1), (1, 3, 1)))
        else:
            time = 0 if kind == 2 else 3
            plan = ((up, (2, time, 1), (0, time, 1)), (down, (0, time, 1), (2, time, 1)))
        found = []
        for side, (partner, there, here) in enumerate(plan):
            exists = partner[0]
            if kind == 2:
                exists = jnp.logical_and(exists, far != 2 * side)
            if kind == 1:
                mine = (1, 1 + side, 1)
            elif kind > 1:
                mine = (1, time, 1)
            device = {"seq": partner[1]}
            send = functools.partial(
                remote,
                block(n, *mine), block(n, *there), (near_s, near_r), (kind, side, n), device
            )
            arrive = functools.partial(
                remote,
                block(n, *mine), block(n, *here), (near_s, near_r), (kind, 1 - side, n), device
            )
            found.append((exists, send, arrive))
        return found

    def diagonal(n):
        device = {"seq": after[1]}
        return remote(
            block(n, far, 2, 1), block(n, far, 0, 1), (near_s, near_r), (4, 0, n), device
        )

    sends_diagonal = jnp.logical_and(after[0], far_exists)
    gets_diagonal = jnp.logical_and(before[0], far_exists)

    def each(kind, n, act):
        for exists, send, arrive in copies(kind, n):

            @pl.when(exists)
            def _():
                act(send, arrive)

    def start(send, arrive):
        send().start()

    greet(partners, peers)
    for_heads(heads, lambda n: start_swap((0, 1), n))

    def forward(n):
        each(0, n, lambda send, arrive: arrive().wait_recv())

        @pl.when(sends_diagonal)
        def _():
            diagonal(n).start()

        for exists_side, kind in ((0, 2), (1, 3)):
            exists, _, arrive = copies(1, n)[exists_side]

            @pl.when(exists)
            def _():
                arrive().wait_recv()
                each(kind, n, start)

    def stage(n):
        wait_swap((0, 1), n)
        each(0, n, start)
        each(1, n, start)
        start_swap((2, 3), n)

        @pl.when(n >= lag)
        def _():
            forward(n - lag)

    lag = min(2, heads)
    for_heads(heads, stage)
    for_heads(lag, lambda n: forward(heads - lag + n))

    def finish(n):
        wait_swap((2, 3), n)
        for array in range(4):
            for j in range(nh - 1):
                swapped(array, n, j, h).wait_send()
        each(0, n, lambda send, arrive: send().wait_send())
        each(1, n, lambda send, arrive: send().wait_send())

        @pl.when(sends_diagonal)
        def _():
            diagonal(n).wait_send()

        @pl.when(gets_diagonal)
        def _():
            diagonal(n).wait_recv()

        for partner, kind in ((before, 2), (after, 3)):

            @pl.when(partner[0])
            def _():
                each(kind, n, lambda send, arrive: (send().wait_send(), arrive().wait_recv()))

    for_heads(heads, finish)


def exchange_in(queries, keys, values, out_grad):
    nh = lax.axis_size("head")
    rows, width = queries.shape
    heads, tile = width // HD // nh, rows * nh // 2
    dma = pltpu.SemaphoreType.DMA
    return pl.pallas_call(
        functools.partial(gather_kernel, nh),
        in_specs=[pl.BlockSpec(memory_space=pl.ANY)] * 4,
        out_specs=[pl.BlockSpec(memory_space=pl.ANY)] * 3,
        out_shape=[
            jax.ShapeDtypeStruct((heads, 2 * tile, HD), jnp.bfloat16),
            jax.ShapeDtypeStruct((heads, 2 * tile, HD), jnp.bfloat16),
            jax.ShapeDtypeStruct((heads, 2, 3, 4, tile, HD), jnp.bfloat16),
        ],
        scratch_shapes=[
            dma((4, heads)),
            dma((4, nh - 1, heads)),
            dma((4, nh - 1, heads)),
            dma((5, 2, heads)),
            dma((5, 2, heads)),
        ],
        compiler_params=pltpu.CompilerParams(collective_id=0, has_side_effects=True),
        name="gather",
    )(queries, keys, values, out_grad)


def scatter_kernel(
    nh,
    dq_in,
    dkv_in,
    dq_out,
    dk_out,
    dv_out,
    mine,
    sides,
    edges,
    times,
    final,
    load,
    own,
    swap_s,
    swap_r,
    near_s,
    near_r,
):
    heads, _, _, _, tile, _ = dkv_in.shape
    rows = dq_out.shape[0]
    h = lax.axis_index("head")
    partners = neighbours()
    up, down, before, after = partners
    peers = [lax.rem(h + j, nh) for j in range(1, nh)]
    senders = [lax.rem(h + nh - j, nh) for j in range(1, nh)]
    outs = (dk_out, dv_out, dq_out)

    def part(array, n, owner):
        span = pl.ds(pl.multiple_of(owner * rows, rows), rows)
        return dq_in.at[n, span] if array == 2 else final.at[n, array, span]

    def columns(array, n, owner):
        start = pl.multiple_of((owner * heads + n) * HD, HD)
        return outs[array].at[:, pl.ds(start, HD)]

    def kept(array, n):
        return pltpu.make_async_copy(part(array, n, h), columns(array, n, h), own.at[array, n])

    def swapped(array, n, j, owner):
        return remote(
            part(array, n, peers[j]),
            columns(array, n, owner),
            (swap_s, swap_r),
            (array, j, n),
            {"head": peers[j]},
        )

    def start_swap(arrays, n):
        for array in arrays:
            for j in range(nh - 1):
                swapped(array, n, j, h).start()
            kept(array, n).start()

    def copies(kind, n):
        if kind == 0:
            plan = ((up, 0), (down, 1))
        else:
            plan = ((before, 0), (after, 1))
        found = []
        for partner, side in plan:
            if kind == 0:
                src, dst, here = dkv_in.at[n, :, 2 * side], sides.at[n, 1 - side], sides.at[n, side]
            else:
                src, dst, here = edges.at[n, side], times.at[n, 1 - side], times.at[n, side]
            device = {"seq": partner[1]}
            send = functools.partial(
                remote, src, dst, (near_s, near_r), (kind, side, n), device)
            arrive = functools.partial(
                remote, src, here, (near_s, near_r), (kind, 1 - side, n), device)
            found.append((partner[0], send, arrive))
        return found

    def each(kind, n, act):
        for exists, send, arrive in copies(kind, n):

            @pl.when(exists)
            def _():
                act(send, arrive)

    def loaded(n):
        return pltpu.make_async_copy(dkv_in.at[n, :, 1], mine.at[n], load.at[n])

    greet(partners, peers)

    def begin(n):
        each(0, n, lambda send, arrive: send().start())
        loaded(n).start()

    for_heads(heads, begin)
    for_heads(heads, lambda n: start_swap((2,), n))
    for buffer, pair in ((sides, (up, down)), (times, (before, after))):
        for side, partner in enumerate(pair):

            @pl.when(jnp.logical_not(partner[0]))
            def _():
                def clear(n):
                    buffer[n, side] = jnp.zeros(buffer.shape[2:], buffer.dtype)

                for_heads(heads, clear)

    def column(n, which, time):
        terms = (mine[n, which, time], sides[n, 0, which, time], sides[n, 1, which, time])
        first, second, third = (term.astype(jnp.float32) for term in terms)
        return first + second + third

    def wrap_up(n):
        each(1, n, lambda send, arrive: arrive().wait_recv())
        for which in range(2):
            for place in range(2):
                total = column(n, which, 1 + place) + times[n, place, which].astype(jnp.float32)
                final[n, which, pl.ds(place * tile, tile)] = total.astype(jnp.bfloat16)
        start_swap((0, 1), n)

    def stage(n):
        each(0, n, lambda send, arrive: arrive().wait_recv())
        loaded(n).wait()
        for which in range(2):
            for side in range(2):
                edges[n, side, which] = column(n, which, 3 * side).astype(jnp.bfloat16)
        each(1, n, lambda send, arrive: send().start())

        @pl.when(n > 0)
        def _():
            wrap_up(n - 1)

    for_heads(heads, stage)
    wrap_up(heads - 1)

    def finish(n):
        for array in range(3):
            for j in range(nh - 1):
                swapped(array, n, j, h).wait_send()
                swapped(array, n, j, senders[j]).wait_recv()
            kept(array, n).wait()
        each(0, n, lambda send, arrive: send().wait_send())
        each(1, n, lambda send, arrive: send().wait_send())

    for_heads(heads, finish)


def exchange_out(dq, dkv):
    nh = lax.axis_size("head")
    heads, rows, _ = dq.shape
    tile = rows // 2
    dma = pltpu.SemaphoreType.DMA
    whole = jax.ShapeDtypeStruct((rows // nh, nh * heads * HD), jnp.bfloat16)

    def held(*shape):
        return pltpu.VMEM(shape + (HD,), jnp.bfloat16)

    return pl.pallas_call(
        functools.partial(scatter_kernel, nh),
        in_specs=[pl.BlockSpec(memory_space=pl.ANY)] * 2,
        out_specs=[pl.BlockSpec(memory_space=pl.ANY)] * 3,
        out_shape=[whole] * 3,
        scratch_shapes=[
            held(heads, 2, 4, tile),
            held(heads, 2, 2, 4, tile),
            held(heads, 2, 2, tile),
            held(heads, 2, 2, tile),
            held(heads, 2, 2 * tile),
            dma((heads,)),
            dma((3, heads)),
            dma((3, nh - 1, heads)),
            dma((3, nh - 1, heads)),
            dma((2, 2, heads)),
            dma((2, 2, heads)),
        ],
        compiler_params=pltpu.CompilerParams(
            collective_id=1, has_side_effects=True, vmem_limit_bytes=44 * 2**20
        ),
        name="scatter",
    )(dq, dkv)


def per_device(queries, keys, values, out_grad, window):
    q, g, kv = exchange_in(queries, keys, values, out_grad)
    dq, dkv = attend(visible_slots(window, q.shape[0]), q, g, kv)
    return exchange_out(dq, dkv)


def solution(mesh):
    rows = P(("seq", "head"), None)
    return jax.shard_map(
        per_device,
        mesh=mesh,
        in_specs=(rows, rows, rows, rows, P()),
        out_specs=(rows, rows, rows),
        check_vma=False,
    )
```

profile of v0, /device:TPU:2, one launch (start us, length us, event | category | flops | bytes accessed | tf_op | source)
XLA Modules:
  0.0 261.7 jit_solution(1164630348984368040)
XLA Ops:
  0.6 0.0 copy-start
  0.7 0.6 copy-done
  1.3 0.1 constant_dynamic-slice_fusion
  1.4 0.1 and_and_fusion
  1.5 0.1 compare_and_fusion
  1.6 0.1 reshape.142.vis_ref
  1.7 100.3 %gather.1 = (bf16[8,768,128]{2,1,0:T(8,128)(2,1)}, bf16[8,768,128]{2,1,0:T(8,128)(2,1)}, bf16[8,2,3,4,384,128]{5,4,3,2,1,0:T(8,128)(2,1)}) custom-call(bf16[384,2048]{1,0:T(8,128)(2,1)} %q_in.1, bf16[384,2048]{1,0:T(8,128)(2,1)} %k_in.1, bf16[384,2048]{1,0:T(8,128)(2,1)} %v_in.1, bf16[384,2048]{1,0:T(8,128)(2,1)} %g_in.1), custom_call_target="tpu_custom_call" | custom-call | tf_op jit(solution)/shard_map/gather/pallas_call | solution.py:379
  102.0 0.0 copy-start.1
  102.0 1.4 copy-done.1
  103.4 0.0 copy-start.2
  103.4 1.4 copy-done.2
  104.9 45.9 %attend.1 = (bf16[8,768,128]{2,1,0:T(8,128)(2,1)S(1)}, bf16[8,2,3,4,384,128]{5,4,3,2,1,0:T(8,128)(2,1)}) custom-call(s32[144]{0:T(256)S(1)} %reshape.142.vis_ref, bf16[8,768,128]{2,1,0:T(8,128)(2,1)S(1)} %copy-done.1, bf16[8,768,128]{2,1,0:T(8,128)(2,1)S(1)} %copy-done.2, bf16[8,2,3,4,384,128]{5,4,3,2,1,0:T(8,128)(2,1)} %get-tuple-element.10.kv_ref), custom_call_target="tpu_custom_call" | custom-call | flops 13589544960 | bytes 42467328 | tf_op jit(solution)/shard_map/attend/pallas_call | solution.py:127
  150.8 107.5 %scatter.1 = (bf16[384,2048]{1,0:T(8,128)(2,1)S(1)}, bf16[384,2048]{1,0:T(8,128)(2,1)S(1)}, bf16[384,2048]{1,0:T(8,128)(2,1)S(1)}) custom-call(bf16[8,768,128]{2,1,0:T(8,128)(2,1)S(1)} %get-tuple-element.11.dq_in, bf16[8,2,3,4,384,128]{5,4,3,2,1,0:T(8,128)(2,1)} %get-tuple-element.12.dkv_in), custom_call_target="tpu_custom_call" | custom-call | tf_op jit(solution)/shard_map/scatter/pallas_call | solution.py:551
  258.3 1.1 copy.11
  259.4 1.1 copy.12
  260.6 1.1 copy.13
  (6 shorter events, 0.1 us)
Async XLA Ops:
  0.6 0.7 copy-start
  102.0 1.4 copy-start.1
  103.4 1.4 copy-start.2
where the time goes:
time: 263 us; the launch traced here: 262 us
  Pallas kernels  254 us (97%)
  local copies, waits for them, and re-layouts  7.03 us (3%)
    pallas_call x1, Pallas kernels, exchange_out(): pl.pallas_call(functools.partial(scatter_kernel, nh), in_specs=[pl.BlockS...  108 us
    pallas_call x1, Pallas kernels, exchange_in(): pl.pallas_call(functools.partial(gather_kernel, nh), in_specs=[pl.BlockSp...  100 us
    pallas_call x1, Pallas kernels, attend(): pl.pallas_call(attend_kernel, grid_spec=pltpu.PrefetchScalarGridSpec(num_...  45.9 us
    unnamed x9, local copies, waits for them, and re-layouts  6.86 us

commit v1 on v0

--- a/solution.py
+++ b/solution.py
@@ -315,7 +315,8 @@
         send().start()
 
     greet(partners, peers)
-    for_heads(heads, lambda n: start_swap((0, 1), n))
+    ahead = min(3, heads)
+    for_heads(ahead, lambda n: start_swap((0, 1), n))
 
     def forward(n):
         each(0, n, lambda send, arrive: arrive().wait_recv())
@@ -336,7 +337,14 @@
         wait_swap((0, 1), n)
         each(0, n, start)
         each(1, n, start)
-        start_swap((2, 3), n)
+
+        @pl.when(n + ahead < heads)
+        def _():
+            start_swap((0, 1), n + ahead)
+
+        @pl.when(n + ahead >= heads)
+        def _():
+            start_swap((2, 3), n + ahead - heads)
 
         @pl.when(n >= lag)
         def _():
@@ -344,6 +352,7 @@
 
     lag = min(2, heads)
     for_heads(heads, stage)
+    for_heads(heads - ahead, lambda n: start_swap((2, 3), ahead + n))
     for_heads(lag, lambda n: forward(heads - lag + n))
 
     def finish(n):
@@ -486,7 +495,8 @@
         each(0, n, lambda send, arrive: send().start())
         loaded(n).start()
 
-    for_heads(heads, begin)
+    ahead = min(3, heads)
+    for_heads(ahead, begin)
     for_heads(heads, lambda n: start_swap((2,), n))
     for buffer, pair in ((sides, (up, down)), (times, (before, after))):
         for side, partner in enumerate(pair):
@@ -518,6 +528,10 @@
             for side in range(2):
                 edges[n, side, which] = column(n, which, 3 * side).astype(jnp.bfloat16)
         each(1, n, lambda send, arrive: send().start())
+
+        @pl.when(n + ahead < heads)
+        def _():
+            begin(n + ahead)
 
         @pl.when(n > 0)
         def _():

time: 263 us -> 260 us (0.989); the launches traced: 262 us -> 255 us
  Pallas kernels: 254 us -> 247 us
    pallas_call x1, Pallas kernels: 108 us -> 100 us  [exchange_out(): pl.pallas_call(functools.partial(scatter_kernel, nh), in_specs=[pl.BlockS...]
where the time goes in v1:
time: 260 us; the launch traced here: 255 us
  Pallas kernels  247 us (95%)
  local copies, waits for them, and re-layouts  7.03 us (3%)
    pallas_call x1, Pallas kernels, exchange_in(): pl.pallas_call(functools.partial(gather_kernel, nh), in_specs=[pl.BlockSp...  100 us
    pallas_call x1, Pallas kernels, exchange_out(): pl.pallas_call(functools.partial(scatter_kernel, nh), in_specs=[pl.BlockS...  100 us
    pallas_call x1, Pallas kernels, attend(): pl.pallas_call(attend_kernel, grid_spec=pltpu.PrefetchScalarGridSpec(num_...  46.8 us
    unnamed x9, local copies, waits for them, and re-layouts  6.86 us

profile of v1, /device:TPU:2, one launch (start us, length us, event | category | flops | bytes accessed | tf_op | source)
XLA Modules:
  0.0 255.3 jit_solution(267607452302511037)
XLA Ops:
  0.6 0.0 copy-start
  0.7 0.6 copy-done
  1.3 0.1 constant_dynamic-slice_fusion
  1.4 0.1 and_and_fusion
  1.5 0.1 compare_and_fusion
  1.6 0.1 reshape.142.vis_ref
  1.7 100.3 %gather.1 = (bf16[8,768,128]{2,1,0:T(8,128)(2,1)}, bf16[8,768,128]{2,1,0:T(8,128)(2,1)}, bf16[8,2,3,4,384,128]{5,4,3,2,1,0:T(8,128)(2,1)}) custom-call(bf16[384,2048]{1,0:T(8,128)(2,1)} %q_in.1, bf16[384,2048]{1,0:T(8,128)(2,1)} %k_in.1, bf16[384,2048]{1,0:T(8,128)(2,1)} %v_in.1, bf16[384,2048]{1,0:T(8,128)(2,1)} %g_in.1), custom_call_target="tpu_custom_call" | custom-call | tf_op jit(solution)/shard_map/gather/pallas_call | solution.py:388
  102.0 0.0 copy-start.1
  102.0 1.4 copy-done.1
  103.4 0.0 copy-start.2
  103.4 1.4 copy-done.2
  104.9 46.8 %attend.1 = (bf16[8,768,128]{2,1,0:T(8,128)(2,1)S(1)}, bf16[8,2,3,4,384,128]{5,4,3,2,1,0:T(8,128)(2,1)}) custom-call(s32[144]{0:T(256)S(1)} %reshape.142.vis_ref, bf16[8,768,128]{2,1,0:T(8,128)(2,1)S(1)} %copy-done.1, bf16[8,768,128]{2,1,0:T(8,128)(2,1)S(1)} %copy-done.2, bf16[8,2,3,4,384,128]{5,4,3,2,1,0:T(8,128)(2,1)} %get-tuple-element.10.kv_ref), custom_call_target="tpu_custom_call" | custom-call | flops 13589544960 | bytes 42467328 | tf_op jit(solution)/shard_map/attend/pallas_call | solution.py:127
  151.6 100.2 %scatter.1 = (bf16[384,2048]{1,0:T(8,128)(2,1)S(1)}, bf16[384,2048]{1,0:T(8,128)(2,1)S(1)}, bf16[384,2048]{1,0:T(8,128)(2,1)S(1)}) custom-call(bf16[8,768,128]{2,1,0:T(8,128)(2,1)S(1)} %get-tuple-element.11.dq_in, bf16[8,2,3,4,384,128]{5,4,3,2,1,0:T(8,128)(2,1)} %get-tuple-element.12.dkv_in), custom_call_target="tpu_custom_call" | custom-call | tf_op jit(solution)/shard_map/scatter/pallas_call | solution.py:565
  251.8 1.1 copy.11
  253.0 1.1 copy.12
  254.1 1.1 copy.13
  (6 shorter events, 0.1 us)
Async XLA Ops:
  0.6 0.7 copy-start
  102.0 1.4 copy-start.1
  103.4 1.4 copy-start.2

commit v2 on v1

--- a/solution.py
+++ b/solution.py
@@ -215,7 +215,7 @@
 
 
 def gather_kernel(
-    nh, q_in, k_in, v_in, g_in, q_out, g_out, kv_out, own, swap_s, swap_r, near_s, near_r
+    nh, q_in, k_in, v_in, g_in, q_out, g_out, kv_out, stage_buf, load, own, swap_s, swap_r, near_s, near_r
 ):
     heads, _, _, _, tile, _ = kv_out.shape
     rows = q_in.shape[0]
@@ -239,22 +239,37 @@
         start = pl.multiple_of((owner * heads + n) * HD, HD)
         return sources[array].at[:, pl.ds(start, HD)]
 
+    def staged(array, n, owner):
+        return stage_buf.at[array, owner * heads + n]
+
+    def loaded(array, n, owner):
+        return pltpu.make_async_copy(
+            columns(array, n, owner), staged(array, n, owner), load.at[array, owner * heads + n]
+        )
+
     def kept(array, n):
-        return pltpu.make_async_copy(columns(array, n, h), place(array, n, h), own.at[array, n])
+        return pltpu.make_async_copy(staged(array, n, h), place(array, n, h), own.at[array, n])
 
     def swapped(array, n, j, owner):
         return remote(
-            columns(array, n, peers[j]),
+            staged(array, n, peers[j]),
             place(array, n, owner),
             (swap_s, swap_r),
             (array, j, n),
             {"head": peers[j]},
         )
 
+    def start_load(arrays, n):
+        for array in arrays:
+            for owner in peers + [h]:
+                loaded(array, n, owner).start()
+
     def start_swap(arrays, n):
         for array in arrays:
             for j in range(nh - 1):
+                loaded(array, n, peers[j]).wait()
                 swapped(array, n, j, h).start()
+            loaded(array, n, h).wait()
             kept(array, n).start()
 
     def wait_swap(arrays, n):
@@ -314,6 +329,8 @@
     def start(send, arrive):
         send().start()
 
+    for_heads(heads, lambda n: start_load((0, 1), n))
+    for_heads(heads, lambda n: start_load((2, 3), n))
     greet(partners, peers)
     ahead = min(3, heads)
     for_heads(ahead, lambda n: start_swap((0, 1), n))
@@ -395,13 +412,17 @@
             jax.ShapeDtypeStruct((heads, 2, 3, 4, tile, HD), jnp.bfloat16),
         ],
         scratch_shapes=[
+            pltpu.VMEM((4, nh * heads, rows, HD), jnp.bfloat16),
+            dma((4, nh * heads)),
             dma((4, heads)),
             dma((4, nh - 1, heads)),
             dma((4, nh - 1, heads)),
             dma((5, 2, heads)),
             dma((5, 2, heads)),
         ],
-        compiler_params=pltpu.CompilerParams(collective_id=0, has_side_effects=True),
+        compiler_params=pltpu.CompilerParams(
+            collective_id=0, has_side_effects=True, vmem_limit_bytes=44 * 2**20
+        ),
         name="gather",
     )(queries, keys, values, out_grad)
 
@@ -418,8 +439,10 @@
     edges,
     times,
     final,
+    landed,
     load,
-    own,
+    pull,
+    push,
     swap_s,
     swap_r,
     near_s,
@@ -442,13 +465,20 @@
         start = pl.multiple_of((owner * heads + n) * HD, HD)
         return outs[array].at[:, pl.ds(start, HD)]
 
-    def kept(array, n):
-        return pltpu.make_async_copy(part(array, n, h), columns(array, n, h), own.at[array, n])
+    def pulled(n):
+        return pltpu.make_async_copy(part(2, n, h), landed.at[2, h * heads + n], pull.at[n])
+
+    def stored(array, n, owner):
+        place = owner * heads + n
+        src = landed.at[array, place]
+        if array < 2 and owner is h:
+            src = part(array, n, h)
+        return pltpu.make_async_copy(src, columns(array, n, owner), push.at[array, place])
 
     def swapped(array, n, j, owner):
         return remote(
             part(array, n, peers[j]),
-            columns(array, n, owner),
+            landed.at[array, owner * heads + n],
             (swap_s, swap_r),
             (array, j, n),
             {"head": peers[j]},
@@ -458,7 +488,19 @@
         for array in arrays:
             for j in range(nh - 1):
                 swapped(array, n, j, h).start()
-            kept(array, n).start()
+            if array == 2:
+                pulled(n).start()
+            else:
+                stored(array, n, h).start()
+
+    def settle(arrays, n):
+        for array in arrays:
+            if array == 2:
+                pulled(n).wait()
+                stored(array, n, h).start()
+            for j in range(nh - 1):
+                swapped(array, n, j, senders[j]).wait_recv()
+                stored(array, n, senders[j]).start()
 
     def copies(kind, n):
         if kind == 0:
@@ -520,6 +562,13 @@
                 total = column(n, which, 1 + place) + times[n, place, which].astype(jnp.float32)
                 final[n, which, pl.ds(place * tile, tile)] = total.astype(jnp.bfloat16)
         start_swap((0, 1), n)
+        settle((2,), n)
+
+        @pl.when(n >= lag)
+        def _():
+            settle((0, 1), n - lag)
+
+    lag = min(2, heads)
 
     def stage(n):
         each(0, n, lambda send, arrive: arrive().wait_recv())
@@ -539,13 +588,14 @@
 
     for_heads(heads, stage)
     wrap_up(heads - 1)
+    for_heads(lag, lambda n: settle((0, 1), heads - lag + n))
 
     def finish(n):
         for array in range(3):
             for j in range(nh - 1):
                 swapped(array, n, j, h).wait_send()
-                swapped(array, n, j, senders[j]).wait_recv()
-            kept(array, n).wait()
+                stored(array, n, senders[j]).wait()
+            stored(array, n, h).wait()
         each(0, n, lambda send, arrive: send().wait_send())
         each(1, n, lambda send, arrive: send().wait_send())
 
@@ -573,8 +623,10 @@
             held(heads, 2, 2, tile),
             held(heads, 2, 2, tile),
             held(heads, 2, 2 * tile),
+            held(3, nh * heads, rows // nh),
             dma((heads,)),
-            dma((3, heads)),
+            dma((heads,)),
+            dma((3, nh * heads)),
             dma((3, nh - 1, heads)),
             dma((3, nh - 1, heads)),
             dma((2, 2, heads)),

time: 260 us -> 253 us (0.973)
  Pallas kernels: 247 us -> 238 us
  local copies, waits for them, and re-layouts: 7.03 us -> 9.85 us
    pallas_call x1, Pallas kernels: 100 us -> 75.7 us  [exchange_in(): pl.pallas_call(functools.partial(gather_kernel, nh), in_specs=[pl.BlockSp...]
    pallas_call x1, Pallas kernels: 46.8 us -> 70.7 us  [attend(): pl.pallas_call(attend_kernel, grid_spec=pltpu.PrefetchScalarGridSpec(num_...]
    pallas_call x1, Pallas kernels: 100 us -> 91.4 us  [exchange_out(): pl.pallas_call(functools.partial(scatter_kernel, nh), in_specs=[pl.BlockS...]
    unnamed x9 -> x13, local copies, waits for them, and re-layouts: 6.86 us -> 9.68 us
where the time goes in v2:
time: 253 us; the launch traced here: 249 us
  Pallas kernels  238 us (94%)
  local copies, waits for them, and re-layouts  9.85 us (4%)
    pallas_call x1, Pallas kernels, exchange_out(): pl.pallas_call(functools.partial(scatter_kernel, nh), in_specs=[pl.BlockS...  91.4 us
    pallas_call x1, Pallas kernels, exchange_in(): pl.pallas_call(functools.partial(gather_kernel, nh), in_specs=[pl.BlockSp...  75.7 us
    pallas_call x1, Pallas kernels, attend(): pl.pallas_call(attend_kernel, grid_spec=pltpu.PrefetchScalarGridSpec(num_...  70.7 us
    unnamed x13, local copies, waits for them, and re-layouts  9.68 us

profile of v2, /device:TPU:2, one launch (start us, length us, event | category | flops | bytes accessed | tf_op | source)
XLA Modules:
  0.0 248.6 jit_solution(14636329541016932038)
XLA Ops:
  0.6 0.0 copy-start
  0.7 0.6 copy-done
  1.3 0.1 constant_dynamic-slice_fusion
  1.4 0.1 and_and_fusion
  1.5 0.1 compare_and_fusion
  1.6 0.1 reshape.142.vis_ref
  1.7 0.0 copy-start.1
  1.7 1.4 copy-done.1
  3.1 0.0 copy-start.2
  3.1 1.4 copy-done.2
  4.5 0.0 copy-start.3
  4.5 1.4 copy-done.3
  5.9 0.0 copy-start.4
  5.9 1.4 copy-done.4
  7.3 75.7 %gather.1 = (bf16[8,768,128]{2,1,0:T(8,128)(2,1)S(1)}, bf16[8,768,128]{2,1,0:T(8,128)(2,1)S(1)}, bf16[8,2,3,4,384,128]{5,4,3,2,1,0:T(8,128)(2,1)}) custom-call(bf16[384,2048]{1,0:T(8,128)(2,1)S(1)} %copy-done.1, bf16[384,2048]{1,0:T(8,128)(2,1)S(1)} %copy-done.2, bf16[384,2048]{1,0:T(8,128)(2,1)S(1)} %copy-done.3, bf16[384,2048]{1,0:T(8,128)(2,1)S(1)} %copy-done.4), custom_call_target="tpu_custom_call" | custom-call | tf_op jit(solution)/shard_map/gather/pallas_call | solution.py:405
  83.0 70.7 %attend.1 = (bf16[8,768,128]{2,1,0:T(8,128)(2,1)S(1)}, bf16[8,2,3,4,384,128]{5,4,3,2,1,0:T(8,128)(2,1)}) custom-call(s32[144]{0:T(256)S(1)} %reshape.142.vis_ref, bf16[8,768,128]{2,1,0:T(8,128)(2,1)S(1)} %get-tuple-element.8.q_ref, bf16[8,768,128]{2,1,0:T(8,128)(2,1)S(1)} %get-tuple-element.9.g_ref, bf16[8,2,3,4,384,128]{5,4,3,2,1,0:T(8,128)(2,1)} %get-tuple-element.10.kv_ref), custom_call_target="tpu_custom_call" | custom-call | flops 13589544960 | bytes 42467328 | tf_op jit(solution)/shard_map/attend/pallas_call | solution.py:127
  153.7 91.4 %scatter.1 = (bf16[384,2048]{1,0:T(8,128)(2,1)S(1)}, bf16[384,2048]{1,0:T(8,128)(2,1)S(1)}, bf16[384,2048]{1,0:T(8,128)(2,1)S(1)}) custom-call(bf16[8,768,128]{2,1,0:T(8,128)(2,1)S(1)} %get-tuple-element.11.dq_in, bf16[8,2,3,4,384,128]{5,4,3,2,1,0:T(8,128)(2,1)} %get-tuple-element.12.dkv_in), custom_call_target="tpu_custom_call" | custom-call | tf_op jit(solution)/shard_map/scatter/pallas_call | solution.py:615
  245.1 1.1 copy.11
  246.3 1.1 copy.12
  247.4 1.1 copy.13
  (6 shorter events, 0.1 us)
Async XLA Ops:
  0.6 0.7 copy-start
  1.7 1.4 copy-start.1
  3.1 1.4 copy-start.2
  4.5 1.4 copy-start.3
  5.9 1.4 copy-start.4

commit v3 on v2

--- a/solution.py
+++ b/solution.py
@@ -440,7 +440,10 @@
     times,
     final,
     landed,
+    crossed,
+    merged,
     load,
+    load_far,
     pull,
     push,
     swap_s,
@@ -456,6 +459,10 @@
     peers = [lax.rem(h + j, nh) for j in range(1, nh)]
     senders = [lax.rem(h + nh - j, nh) for j in range(1, nh)]
     outs = (dk_out, dv_out, dq_out)
+    far_exists, far = far_row()
+    far_side = lax.div(far, 2)
+    sends_cross = jnp.logical_and(before[0], far_exists)
+    gets_cross = jnp.logical_and(after[0], far_exists)
 
     def part(array, n, owner):
         span = pl.ds(pl.multiple_of(owner * rows, rows), rows)
@@ -509,7 +516,9 @@
             plan = ((before, 0), (after, 1))
         found = []
         for partner, side in plan:
+            exists = partner[0]
             if kind == 0:
+                exists = jnp.logical_and(exists, far_side != side)
                 src, dst, here = dkv_in.at[n, :, 2 * side], sides.at[n, 1 - side], sides.at[n, side]
             else:
                 src, dst, here = edges.at[n, side], times.at[n, 1 - side], times.at[n, side]
@@ -518,7 +527,7 @@
                 remote, src, dst, (near_s, near_r), (kind, side, n), device)
             arrive = functools.partial(
                 remote, src, here, (near_s, near_r), (kind, 1 - side, n), device)
-            found.append((partner[0], send, arrive))
+            found.append((exists, send, arrive))
         return found
 
     def each(kind, n, act):
@@ -531,13 +540,54 @@
     def loaded(n):
         return pltpu.make_async_copy(dkv_in.at[n, :, 1], mine.at[n], load.at[n])
 
+    def loaded_far(n):
+        return pltpu.make_async_copy(dkv_in.at[n, :, far, 2], merged.at[n], load_far.at[n])
+
+    def across(n, k, side):
+        time = (1, 3, 2)[k]
+        src = merged.at[n] if k == 2 else dkv_in.at[n, :, far, time]
+        device = {"seq": lax.axis_index("seq") + far - 1}
+        index = (2 + k // 2, k % 2, n)
+        return remote(src, sides.at[n, side, :, time], (near_s, near_r), index, device)
+
+    def cross(n):
+        device = {"seq": before[1]}
+        return remote(
+            dkv_in.at[n, :, far, 0], crossed.at[n], (near_s, near_r), (3, 1, n), device
+        )
+
     greet(partners, peers)
 
     def begin(n):
+        @pl.when(sends_cross)
+        def _():
+            cross(n).start()
+
         each(0, n, lambda send, arrive: send().start())
         loaded(n).start()
 
-    ahead = min(3, heads)
+        @pl.when(far_exists)
+        def _():
+            loaded_far(n).start()
+            across(n, 0, 1 - far_side).start()
+            across(n, 1, 1 - far_side).start()
+
+    def merge(n):
+        @pl.when(far_exists)
+        def _():
+            loaded_far(n).wait()
+
+        @pl.when(gets_cross)
+        def _():
+            cross(n).wait_recv()
+            total = merged[n].astype(jnp.float32) + crossed[n].astype(jnp.float32)
+            merged[n] = total.astype(jnp.bfloat16)
+
+        @pl.when(far_exists)
+        def _():
+            across(n, 2, 1 - far_side).start()
+
+    ahead = min(4, heads)
     for_heads(ahead, begin)
     for_heads(heads, lambda n: start_swap((2,), n))
     for buffer, pair in ((sides, (up, down)), (times, (before, after))):
@@ -549,6 +599,11 @@
                     buffer[n, side] = jnp.zeros(buffer.shape[2:], buffer.dtype)
 
                 for_heads(heads, clear)
+
+    def clear_far(n):
+        sides[n, far_side, :, 0] = jnp.zeros(merged.shape[1:], merged.dtype)
+
+    for_heads(heads, clear_far)
 
     def column(n, which, time):
         terms = (mine[n, which, time], sides[n, 0, which, time], sides[n, 1, which, time])
@@ -573,21 +628,35 @@
     def stage(n):
         each(0, n, lambda send, arrive: arrive().wait_recv())
         loaded(n).wait()
+
+        @pl.when(far_exists)
+        def _():
+            for k in range(3):
+                across(n, k, far_side).wait_recv()
+
         for which in range(2):
             for side in range(2):
                 edges[n, side, which] = column(n, which, 3 * side).astype(jnp.bfloat16)
         each(1, n, lambda send, arrive: send().start())
 
+    def step(n):
+        merge(n)
+
         @pl.when(n + ahead < heads)
         def _():
             begin(n + ahead)
 
-        @pl.when(n > 0)
-        def _():
-            wrap_up(n - 1)
-
-    for_heads(heads, stage)
-    wrap_up(heads - 1)
+        @pl.when(n >= 1)
+        def _():
+            stage(n - 1)
+
+        @pl.when(n >= 2)
+        def _():
+            wrap_up(n - 2)
+
+    for_heads(heads, step)
+    stage(heads - 1)
+    for_heads(lag, lambda n: wrap_up(heads - lag + n))
     for_heads(lag, lambda n: settle((0, 1), heads - lag + n))
 
     def finish(n):
@@ -598,6 +667,15 @@
             stored(array, n, h).wait()
         each(0, n, lambda send, arrive: send().wait_send())
         each(1, n, lambda send, arrive: send().wait_send())
+
+        @pl.when(sends_cross)
+        def _():
+            cross(n).wait_send()
+
+        @pl.when(far_exists)
+        def _():
+            for k in range(3):
+                across(n, k, 1 - far_side).wait_send()
 
     for_heads(heads, finish)
 
@@ -624,13 +702,16 @@
             held(heads, 2, 2, tile),
             held(heads, 2, 2 * tile),
             held(3, nh * heads, rows // nh),
+            held(heads, 2, tile),
+            held(heads, 2, tile),
+            dma((heads,)),
             dma((heads,)),
             dma((heads,)),
             dma((3, nh * heads)),
             dma((3, nh - 1, heads)),
             dma((3, nh - 1, heads)),
-            dma((2, 2, heads)),
-            dma((2, 2, heads)),
+            dma((4, 2, heads)),
+            dma((4, 2, heads)),
         ],
         compiler_params=pltpu.CompilerParams(
             collective_id=1, has_side_effects=True, vmem_limit_bytes=44 * 2**20

time: 253 us -> 237 us (0.937); the launches traced: 249 us -> 236 us
  Pallas kernels: 238 us -> 226 us
    pallas_call x1, Pallas kernels: 91.4 us -> 78.4 us  [exchange_out(): pl.pallas_call(functools.partial(scatter_kernel, nh), in_specs=[pl.BlockS...]
where the time goes in v3:
time: 237 us; the launch traced here: 236 us
  Pallas kernels  226 us (95%)
  local copies, waits for them, and re-layouts  9.85 us (4%)
    pallas_call x1, Pallas kernels, exchange_out(): pl.pallas_call(functools.partial(scatter_kernel, nh), in_specs=[pl.BlockS...  78.4 us
    pallas_call x1, Pallas kernels, exchange_in(): pl.pallas_call(functools.partial(gather_kernel, nh), in_specs=[pl.BlockSp...  75.7 us
    pallas_call x1, Pallas kernels, attend(): pl.pallas_call(attend_kernel, grid_spec=pltpu.PrefetchScalarGridSpec(num_...  71.5 us
    unnamed x13, local copies, waits for them, and re-layouts  9.68 us

profile of v3, /device:TPU:2, one launch (start us, length us, event | category | flops | bytes accessed | tf_op | source)
XLA Modules:
  0.0 236.4 jit_solution(106718261868793414)
XLA Ops:
  0.6 0.0 copy-start
  0.7 0.6 copy-done
  1.3 0.1 constant_dynamic-slice_fusion
  1.4 0.1 and_and_fusion
  1.5 0.1 compare_and_fusion
  1.6 0.1 reshape.142.vis_ref
  1.7 0.0 copy-start.1
  1.7 1.4 copy-done.1
  3.1 0.0 copy-start.2
  3.1 1.4 copy-done.2
  4.5 0.0 copy-start.3
  4.5 1.4 copy-done.3
  5.9 0.0 copy-start.4
  5.9 1.4 copy-done.4
  7.3 75.7 %gather.1 = (bf16[8,768,128]{2,1,0:T(8,128)(2,1)S(1)}, bf16[8,768,128]{2,1,0:T(8,128)(2,1)S(1)}, bf16[8,2,3,4,384,128]{5,4,3,2,1,0:T(8,128)(2,1)}) custom-call(bf16[384,2048]{1,0:T(8,128)(2,1)S(1)} %copy-done.1, bf16[384,2048]{1,0:T(8,128)(2,1)S(1)} %copy-done.2, bf16[384,2048]{1,0:T(8,128)(2,1)S(1)} %copy-done.3, bf16[384,2048]{1,0:T(8,128)(2,1)S(1)} %copy-done.4), custom_call_target="tpu_custom_call" | custom-call | tf_op jit(solution)/shard_map/gather/pallas_call | solution.py:405
  83.0 71.5 %attend.1 = (bf16[8,768,128]{2,1,0:T(8,128)(2,1)S(1)}, bf16[8,2,3,4,384,128]{5,4,3,2,1,0:T(8,128)(2,1)}) custom-call(s32[144]{0:T(256)S(1)} %reshape.142.vis_ref, bf16[8,768,128]{2,1,0:T(8,128)(2,1)S(1)} %get-tuple-element.8.q_ref, bf16[8,768,128]{2,1,0:T(8,128)(2,1)S(1)} %get-tuple-element.9.g_ref, bf16[8,2,3,4,384,128]{5,4,3,2,1,0:T(8,128)(2,1)} %get-tuple-element.10.kv_ref), custom_call_target="tpu_custom_call" | custom-call | flops 13589544960 | bytes 42467328 | tf_op jit(solution)/shard_map/attend/pallas_call | solution.py:127
  154.6 78.4 %scatter.1 = (bf16[384,2048]{1,0:T(8,128)(2,1)S(1)}, bf16[384,2048]{1,0:T(8,128)(2,1)S(1)}, bf16[384,2048]{1,0:T(8,128)(2,1)S(1)}) custom-call(bf16[8,768,128]{2,1,0:T(8,128)(2,1)S(1)} %get-tuple-element.11.dq_in, bf16[8,2,3,4,384,128]{5,4,3,2,1,0:T(8,128)(2,1)} %get-tuple-element.12.dkv_in), custom_call_target="tpu_custom_call" | custom-call | tf_op jit(solution)/shard_map/scatter/pallas_call | solution.py:693
  232.9 1.1 copy.11
  234.1 1.1 copy.12
  235.2 1.1 copy.13
  (6 shorter events, 0.1 us)
Async XLA Ops:
  0.6 0.7 copy-start
  1.7 1.4 copy-start.1
  3.1 1.4 copy-start.2
  4.5 1.4 copy-start.3
  5.9 1.4 copy-start.4

commit v4 on v3

--- a/solution.py
+++ b/solution.py
@@ -56,39 +56,64 @@
         dqt[...] = jnp.zeros_like(dqt)
 
         def over_visible(body):
-            def step(slot, carry):
-                @pl.when(vis_ref[(head * 2 + qt) * 9 + slot] == 1)
+            def by_row(row, carry):
+                first = (head * 2 + qt) * 9 + row
+                parts = [vis_ref[first + 3 * step] for step in range(3)]
+                full = parts[0] + parts[1] + parts[2] == 3
+
+                @pl.when(full)
                 def _():
-                    body(slot, lax.rem(slot, 3), qt + lax.div(slot, 3))
+                    body(row * 3, row, qt, 3)
+
+                @pl.when(jnp.logical_not(full))
+                def _():
+                    def single(step, carry):
+                        @pl.when(vis_ref[first + 3 * step] == 1)
+                        def _():
+                            body(row * 3 + step, row, qt + step, 1)
+
+                        return carry
+
+                    lax.fori_loop(0, 3, single, 0)
 
                 return carry
 
-            lax.fori_loop(0, 9, step, 0)
-
-        def scores(slot, row, time):
-            s = dot(kv_ref[0, 0, row, time], q, ((1,), (1,)))
+            lax.fori_loop(0, 3, by_row, 0)
+
+        def near(which, row, time, span):
+            return kv_ref[0, which, row, pl.ds(time, span)].reshape(span * tile, HD)
+
+        def scores(slot, row, time, span):
+            s = dot(near(0, row, time, span), q, ((1,), (1,)))
             old = top[...]
             new = jnp.maximum(old, jnp.max(s, axis=0, keepdims=True))
             shrink = jnp.exp2((old - new) * (SCALE * LOG2E))
-            dp = dot(kv_ref[0, 1, row, time], g, ((1,), (1,)))
+            dp = dot(near(1, row, time, span), g, ((1,), (1,)))
             e = jnp.exp2((s - new) * (SCALE * LOG2E))
-            e_scr[slot] = e
-            dp_scr[slot] = dp
+            e_scr[pl.ds(slot, span)] = e.reshape(span, tile, tile)
+            dp_scr[pl.ds(slot, span)] = dp.reshape(span, tile, tile)
             tops[slot] = new
             top[...] = new
             total[...] = total[...] * shrink + jnp.sum(e, axis=0, keepdims=True)
             delta[...] = delta[...] * shrink + jnp.sum(e * dp, axis=0, keepdims=True)
 
-        def grads(slot, row, time):
-            @pl.when(jnp.logical_or(qt == 0, jnp.logical_not(seen(0, row, time))))
-            def _():
-                acc[:, row, time] = jnp.zeros((2,) + acc.shape[3:], jnp.float32)
-
-            p = e_scr[slot] * (jnp.exp2((tops[slot] - top[...]) * (SCALE * LOG2E)) * total[...])
-            ds = (p * (dp_scr[slot] - delta[...])).astype(jnp.bfloat16)
-            acc[1, row, time] += dot(p.astype(jnp.bfloat16), g, ((1,), (0,)))
-            acc[0, row, time] += dot(ds, q, ((1,), (0,)))
-            dqt[...] += dot(kv_ref[0, 0, row, time], ds, ((0,), (0,)))
+        def grads(slot, row, time, span):
+            for step in range(span):
+
+                @pl.when(jnp.logical_or(qt == 0, jnp.logical_not(seen(0, row, time + step))))
+                def _():
+                    acc[:, row, time + step] = jnp.zeros((2,) + acc.shape[3:], jnp.float32)
+
+            def flat(ref):
+                return ref[pl.ds(slot, span)].reshape(span * tile, tile)
+
+            times = pl.ds(time, span)
+            shape = (span, tile, HD)
+            p = flat(e_scr) * (jnp.exp2((tops[slot] - top[...]) * (SCALE * LOG2E)) * total[...])
+            ds = (p * (flat(dp_scr) - delta[...])).astype(jnp.bfloat16)
+            acc[1, row, times] += dot(p.astype(jnp.bfloat16), g, ((1,), (0,))).reshape(shape)
+            acc[0, row, times] += dot(ds, q, ((1,), (0,))).reshape(shape)
+            dqt[...] += dot(near(0, row, time, span), ds, ((0,), (0,)))
 
         over_visible(scores)
         total[...] = 1.0 / total[...]

time: 237 us -> 227 us (0.958)
  Pallas kernels: 226 us -> 214 us
    pallas_call x1, Pallas kernels: 78.4 us -> 70.3 us  [exchange_out(): pl.pallas_call(functools.partial(scatter_kernel, nh), in_specs=[pl.BlockS...]
    pallas_call x1, Pallas kernels: 71.5 us -> 68.3 us  [attend(): pl.pallas_call(attend_kernel, grid_spec=pltpu.PrefetchScalarGridSpec(num_...]
where the time goes in v4:
time: 227 us; the launch traced here: 225 us
  Pallas kernels  214 us (94%)
  local copies, waits for them, and re-layouts  9.85 us (4%)
    pallas_call x1, Pallas kernels, exchange_in(): pl.pallas_call(functools.partial(gather_kernel, nh), in_specs=[pl.BlockSp...  75.7 us
    pallas_call x1, Pallas kernels, exchange_out(): pl.pallas_call(functools.partial(scatter_kernel, nh), in_specs=[pl.BlockS...  70.3 us
    pallas_call x1, Pallas kernels, attend(): pl.pallas_call(attend_kernel, grid_spec=pltpu.PrefetchScalarGridSpec(num_...  68.3 us
    unnamed x13, local copies, waits for them, and re-layouts  9.68 us

profile of v4, /device:TPU:2, one launch (start us, length us, event | category | flops | bytes accessed | tf_op | source)
XLA Modules:
  0.0 225.1 jit_solution(8028364821637565482)
XLA Ops:
  0.6 0.0 copy-start
  0.7 0.6 copy-done
  1.3 0.1 constant_dynamic-slice_fusion
  1.4 0.1 and_and_fusion
  1.5 0.1 compare_and_fusion
  1.6 0.1 reshape.142.vis_ref
  1.7 0.0 copy-start.1
  1.7 1.4 copy-done.1
  3.1 0.0 copy-start.2
  3.1 1.4 copy-done.2
  4.5 0.0 copy-start.3
  4.5 1.4 copy-done.3
  5.9 0.0 copy-start.4
  5.9 1.4 copy-done.4
  7.3 75.7 %gather.1 = (bf16[8,768,128]{2,1,0:T(8,128)(2,1)S(1)}, bf16[8,768,128]{2,1,0:T(8,128)(2,1)S(1)}, bf16[8,2,3,4,384,128]{5,4,3,2,1,0:T(8,128)(2,1)}) custom-call(bf16[384,2048]{1,0:T(8,128)(2,1)S(1)} %copy-done.1, bf16[384,2048]{1,0:T(8,128)(2,1)S(1)} %copy-done.2, bf16[384,2048]{1,0:T(8,128)(2,1)S(1)} %copy-done.3, bf16[384,2048]{1,0:T(8,128)(2,1)S(1)} %copy-done.4), custom_call_target="tpu_custom_call" | custom-call | tf_op jit(solution)/shard_map/gather/pallas_call | solution.py:430
  83.0 68.3 %attend.1 = (bf16[8,768,128]{2,1,0:T(8,128)(2,1)S(1)}, bf16[8,2,3,4,384,128]{5,4,3,2,1,0:T(8,128)(2,1)}) custom-call(s32[144]{0:T(256)S(1)} %reshape.142.vis_ref, bf16[8,768,128]{2,1,0:T(8,128)(2,1)S(1)} %get-tuple-element.8.q_ref, bf16[8,768,128]{2,1,0:T(8,128)(2,1)S(1)} %get-tuple-element.9.g_ref, bf16[8,2,3,4,384,128]{5,4,3,2,1,0:T(8,128)(2,1)} %get-tuple-element.10.kv_ref), custom_call_target="tpu_custom_call" | custom-call | flops 13589544960 | bytes 42467328 | tf_op jit(solution)/shard_map/attend/pallas_call | solution.py:152
  151.3 70.3 %scatter.1 = (bf16[384,2048]{1,0:T(8,128)(2,1)S(1)}, bf16[384,2048]{1,0:T(8,128)(2,1)S(1)}, bf16[384,2048]{1,0:T(8,128)(2,1)S(1)}) custom-call(bf16[8,768,128]{2,1,0:T(8,128)(2,1)S(1)} %get-tuple-element.11.dq_in, bf16[8,2,3,4,384,128]{5,4,3,2,1,0:T(8,128)(2,1)} %get-tuple-element.12.dkv_in), custom_call_target="tpu_custom_call" | custom-call | tf_op jit(solution)/shard_map/scatter/pallas_call | solution.py:718
  221.7 1.1 copy.11
  222.8 1.1 copy.12
  224.0 1.1 copy.13
  (6 shorter events, 0.1 us)
Async XLA Ops:
  0.6 0.7 copy-start
  1.7 1.4 copy-start.1
  3.1 1.4 copy-start.2
  4.5 1.4 copy-start.3
  5.9 1.4 copy-start.4
